TPU v7x, 256 devices: a whole 4x4x8 slice. The times are simulated.
256 devices in a mesh: rep: 32 (over z_hi, y, core), fsdp: 8 (over z_lo, x).
Axes of the slice: x: 4, y: 4, z: 8 (z_hi: 4, z_lo: 2; z = z_hi * 2 + z_lo), core: 2. Of those that a mesh axis runs over, the one named last changes fastest.
Arguments:
- gradients: bfloat16 [32, 8, 4, 64, 5120], P('rep', 'fsdp'), may hold values from -6 to 6
- momentum: float32 [32, 4, 64, 5120], P('rep', None, 'fsdp'), may hold values from -45 to 45
Outputs:
- new_momentum: float32 [32, 4, 64, 5120], P('rep', None, 'fsdp')
- update: float32 [4, 64, 5120], P(None, 'fsdp')
All inputs are finite; a program needn't handle non-finite values.
Results may differ from a plain program's by a relative error of at most 0.0003.
Values sent between devices are 32-bit elements; how exact they have to be, the bound alone decides.
A program may use at most 64 MiB of HBM per device.

v0:
```python
import jax
import jax.numpy as jnp
import ml_dtypes
import numpy as np
from jax import lax
from jax.experimental import pallas as pl
from jax.experimental.pallas import tpu as pltpu
from jax.sharding import PartitionSpec as P

D, MATS, GROUP, KEEP, ROWS = 5120, 4, 64, 8, 64
BETA, EPS = 0.999, 1e-06
NX, NY, NZL, NZH, NC, N_REP = 4, 4, 2, 4, 2, 32
OWN = 8
LANES = 128
TILES = 8
SPAN = LANES * TILES
GROUPS = D // SPAN
HIGH = 7 * LANES
LOW = GROUPS * LANES
GRAD = MATS * ROWS
MINE = MATS * OWN
WIDE = 4 * LANES

F32, BF16 = jnp.float32, jnp.bfloat16
MESH = pl.DeviceIdType.MESH


def split(table):
    high = table.astype(ml_dtypes.bfloat16)
    low = (table - high.astype(np.float64)).astype(ml_dtypes.bfloat16)
    return high, low


def tables():
    n, k = np.arange(GROUP), np.arange(GROUP)[:, None]
    basis = np.sqrt(2.0 / GROUP) * np.cos(np.pi * (n + 0.5) * k / GROUP)
    basis[0] *= np.sqrt(0.5)
    rest = GROUP - KEEP
    high = np.zeros((LANES, 2 * rest))
    for b in range(2):
        high[b * GROUP : (b + 1) * GROUP, b * rest : (b + 1) * rest] = basis[KEEP:].T
    forward = np.zeros((7, 2 * LANES, LANES))
    for t in range(7):
        forward[t, :LANES, : 2 * rest] = high
        forward[t, LANES:, 2 * rest :] = high[:, 16 * t : 16 * t + 16]
    inverse = np.zeros((7, LANES, 2 * LANES))
    for t in range(7):
        inverse[t] = forward[t].T
    blocks = SPAN // GROUP
    keep = np.zeros((SPAN, LANES))
    mean = np.zeros((LANES, SPAN))
    for c in range(blocks):
        keep[c * GROUP : (c + 1) * GROUP, c * KEEP : (c + 1) * KEEP] = basis[:KEEP].T
        mean[c * KEEP : (c + 1) * KEEP, c * GROUP : (c + 1) * GROUP] = 1.0 / GROUP
    both = lambda table: np.concatenate(split(table), axis=-1)
    wide = np.concatenate([both(forward).reshape(-1, 2 * LANES), both(keep)], axis=0)
    back = np.concatenate([both(keep.T), mean.astype(ml_dtypes.bfloat16)], axis=-1)
    back = back.reshape(LANES, 6, WIDE).transpose(1, 0, 2).reshape(-1, WIDE)
    return wide, np.concatenate([both(inverse).reshape(-1, WIDE), back], axis=0)


def halves(value):
    top = value.astype(BF16)
    return top, (value - top.astype(F32)).astype(BF16)


def dot(a, b):
    return jnp.dot(a, b, preferred_element_type=F32)


X_UNITS = [(2, 0), (2, 2), (3, 0), (3, 2), (4, 0), (4, 2)]
Z_UNITS = [(0, 0), (0, 2), (1, 0), (1, 2)]
SENDS = ["x2", "xa", "xb", "xz", "z4", "z2", "za", "zb", "la", "lc", "ld", "lf"]
PLAN = [
    ("F", 4), ("XS", 4), ("F", 1), ("ZS", 3), ("FL", 4), ("FL", 3),
    ("XS", 5), ("FL", 2), ("FL", 1), ("FL", 0), ("LA", 0), ("F", 3),
    ("XS", 2), ("ZS", 2), ("F", 2), ("XS", 0), ("F", 0), ("XS", 3),
    ("XP", 5), ("ZS", 1), ("ZS", 0), ("XP", 2), ("LC", 0), ("XS", 1),
    ("XP", 3), ("XP", 4), ("ZC", 3), ("XP", 0), ("ZC", 1), ("LD", 0),
    ("ZC", 2), ("XP", 1), ("XC", 2), ("XC", 3), ("XC", 5), ("XC", 4),
    ("ZP", 3), ("ZC", 0), ("XE", 2), ("ZP", 2), ("XE", 3), ("BK", 3),
    ("XC", 0), ("XE", 5), ("LF", 0), ("ZP", 1), ("XC", 1), ("XE", 4),
    ("BK", 4), ("ZP", 0), ("ZE", 3), ("ZE", 2), ("BK", 1), ("XE", 1),
    ("XE", 0), ("BK", 2), ("ZE", 1), ("ZE", 0), ("BK", 0), ("N", 3),
    ("N", 1), ("N", 2), ("N", 0), ("N", 4),
]


def kernel(
    grads, momentum, wide_hbm, back_hbm, new_out, upd_out,
    xin, mom, wide, back, sx, sz, lw,
    xr2, xab, xrz, zr4, zr2, zab,
    la, lc, le, es, total, nm, up,
    load_sem, store_sem, send_sem, recv_sem, column_sem, stack_sem,
):
    rep, fsdp = lax.axis_index("rep"), lax.axis_index("fsdp")
    core, y, zh = lax.rem(rep, 2), lax.rem(lax.div(rep, 2), 4), lax.div(rep, 8)
    x, z = lax.rem(fsdp, 4), lax.div(fsdp, 4)

    def ring(v, d):
        return lax.rem(v + (d + 4), 4)

    xs, ys, zs = ([v] + [ring(v, d) for d in (1, 2, 3)] for v in (x, y, zh))
    other_core, other_z = 1 - core, 1 - z
    own_rep, own_fsdp = rep, fsdp
    places = {}

    def device(dzh=0, dy=0, dcore=0, dz=0, dx=0):
        key = (dzh, dy % 4, dcore, dz, dx % 4)
        if key not in places:
            c2, z2 = other_core if dcore else core, other_z if dz else z
            moved = dzh or dy or dcore
            r2 = (zs[dzh] * 4 + ys[dy % 4]) * 2 + c2 if moved else own_rep
            places[key] = (r2, z2 * 4 + xs[dx % 4] if dz or dx else own_fsdp)
        return places[key]

    for dy in range(4):
        for dc in range(2):
            device(dy=dy, dcore=dc)
    for d in range(4):
        for dz in range(2):
            device(dzh=d, dz=dz)
        device(dx=d)

    column = [(dy, dc) for dy in range(4) for dc in range(2) if dy or dc]
    barrier = pltpu.get_barrier_semaphore()

    def greet(sem, p):
        pl.semaphore_signal(sem, inc=1, device_id=p, device_id_type=MESH)

    def later_in_column(dy, dc):
        if dy:
            return ring(y, dy) > y
        return core == 1

    def later_in_stack(d):
        return ring(zh, d) > zh

    def greet_others(sem_of, later):
        def where(test, sem, places):
            @pl.when(test if later else jnp.logical_not(test))
            def _():
                for place in places:
                    greet(sem, place)

        for d in range(4):
            cores = range(2) if d else (1,)
            where(later_in_column(d, 1), sem_of[0], [device(dy=d, dcore=dc) for dc in cores])
        for d in (1, 2, 3):
            where(later_in_stack(d), sem_of[1], [device(dzh=d, dz=dz) for dz in range(2)])

    for d in (1, 2, 3):
        greet(barrier, device(dx=d))
    greet(barrier, device(dz=1))
    column_later = 2 * (3 - y) + core
    stack_later = 2 * (3 - zh)

    def enter():
        pl.semaphore_wait(barrier, 4 + (7 - column_later) + (6 - stack_later))
    def remote(kind, src, dst, to, recv):
        return pltpu.make_async_remote_copy(
            src_ref=src, dst_ref=dst, send_sem=send_sem.at[SENDS.index(kind)],
            recv_sem=recv_sem.at[recv], device_id=to, device_id_type=MESH,
        )

    def send(kind, src, dst, to, recv):
        remote(kind, src, dst, to, recv).start()

    def await_bytes(ref, sem):
        pltpu.make_async_copy(ref, ref, sem).wait()

    def received(ref, recv):
        await_bytes(ref, recv_sem.at[recv])

    def all_sent(kind, ref):
        await_bytes(ref, send_sem.at[SENDS.index(kind)])

    loads = []

    def load(src, dst):
        copy = pltpu.make_async_copy(src, dst, load_sem.at[len(loads)])
        copy.start()
        loads.append(copy)
        return copy

    waited = set()

    def arrived(copy):
        if id(copy) not in waited:
            waited.add(id(copy))
            copy.wait()

    def load_group(g):
        cols = pl.ds(g * SPAN, SPAN)
        return load(momentum.at[:, cols], mom.at[:, cols]), load(grads.at[:, cols], xin.at[pl.ds(0, GRAD), cols])

    order = [g for name, g in PLAN if name == "F"]
    front = pl.ds(0, 7 * 2 * LANES)
    rest = pl.ds(7 * 2 * LANES, SPAN)
    group_loads = {order[0]: load_group(order[0])}
    load_wide = load(wide_hbm.at[front], wide.at[front])
    load_rest = []
    greet_others((barrier, barrier), True)

    def load_others():
        for g in order[1:]:
            group_loads[g] = load_group(g)
        load_rest.append(load(wide_hbm.at[rest], wide.at[rest]))
        load_rest.append(load(back_hbm, back))

    ready = set()

    def prepare(g):
        if g not in ready:
            ready.add(g)
            for copy in group_loads[g]:
                copy.wait()
            cols = slice(g * SPAN, (g + 1) * SPAN)
            top, low_part = halves(BETA * mom[:, cols])
            xin[GRAD : GRAD + MINE, cols] = top
            xin[GRAD + MINE :, cols] = low_part

    def fold(v):
        v = v[:, :LANES] + v[:, LANES:]
        own = v[GRAD : GRAD + MINE] + v[GRAD + MINE :]
        return v[:GRAD].reshape(MATS, NZL, NX, OWN, LANES), own.reshape(MATS, OWN, LANES)

    def forward(g):
        prepare(g)
        arrived(load_wide)
        if not load_rest:
            load_others()
        base = g * SPAN
        last = xin[:, base + HIGH : base + SPAN]
        for t in range(7):
            both = jnp.concatenate([xin[:, base + t * LANES : base + (t + 1) * LANES], last], axis=1)
            value, own = fold(dot(both, wide[t * 2 * LANES : (t + 1) * 2 * LANES]))
            lanes = slice(t * LANES, (t + 1) * LANES)
            for h in range(2):
                mats = slice(2 * h, 2 * h + 2)
                if (g, 2 * h) in X_UNITS:
                    u = X_UNITS.index((g, 2 * h))
                    for m in range(2):
                        for k in range(NZL):
                            sx[u, :, k, m, :, lanes] = value[2 * h + m, k]
                    sx[u, x, z, :, :, lanes] += own[mats]
                else:
                    u = Z_UNITS.index((g, 2 * h))
                    for m in range(2):
                        for k in range(NZL):
                            sz[u, k, :, m, :, lanes] = value[2 * h + m, k]
                    sz[u, z, x, :, :, lanes] += own[mats]

    def forward_low(g):
        prepare(g)
        arrived(load_rest[0])
        value, own = fold(dot(xin[:, g * SPAN : (g + 1) * SPAN], wide[7 * 2 * LANES :]))
        lanes = slice(g * LANES, (g + 1) * LANES)
        lw[:, :, :, :, lanes] = value
        lw[:, z, x, :, lanes] += own

    way = lambda u: 1 if u % 2 == 0 else -1
    z_way = lambda u: -way(u)
    nx, nz = len(X_UNITS), len(Z_UNITS)
    X2, XAB, XZ = 0, nx, 2 * nx
    Z4, Z2, ZAB = 3 * nx, 3 * nx + nz, 3 * nx + 2 * nz
    LOW_A = 3 * nx + 3 * nz
    LOW_C, LOW_D, LOW_F = LOW_A + 1, LOW_A + 2, LOW_A + 3

    def x_start(u):
        d = way(u)
        send("x2", sx.at[u, xs[2]], xr2.at[u], device(dx=d), X2 + u)
        send("xa", sx.at[u, xs[-d]], xab.at[u, 0], device(dx=-d), XAB + u)

    def x_pass(u):
        d = way(u)
        received(xr2.at[u], X2 + u)
        sx[u, xs[d]] += xr2[u]
        send("xb", sx.at[u, xs[d]], xab.at[u, 1], device(dx=d), XAB + u)

    def x_cross(u):
        received(xab.at[u], XAB + u)
        sx[u, x] += xab[u, 0] + xab[u, 1]
        send("xz", sx.at[u, x, other_z], xrz.at[u], device(dz=1), XZ + u)

    def z_start(u):
        send("z4", sz.at[u, other_z], zr4.at[u], device(dz=1), Z4 + u)

    def z_cross(u):
        d = z_way(u)
        received(zr4.at[u], Z4 + u)
        sz[u, z] += zr4[u]
        send("z2", sz.at[u, z, xs[2]], zr2.at[u], device(dx=d), Z2 + u)
        send("za", sz.at[u, z, xs[-d]], zab.at[u, 0], device(dx=-d), ZAB + u)

    def z_pass(u):
        d = z_way(u)
        received(zr2.at[u], Z2 + u)
        sz[u, z, xs[d]] += zr2[u]
        send("zb", sz.at[u, z, xs[d]], zab.at[u, 1], device(dx=d), ZAB + u)

    parts = {}

    def x_end(u):
        received(xrz.at[u], XZ + u)
        parts[X_UNITS[u]] = sx[u, x, z] + xrz[u]

    def z_end(u):
        received(zab.at[u], ZAB + u)
        parts[Z_UNITS[u]] = sz[u, z, x] + (zab[u, 0] + zab[u, 1])

    stores = []

    def store(src, dst):
        copy = pltpu.make_async_copy(src, dst, store_sem.at[len(stores)])
        copy.start()
        stores.append(copy)

    def backward(g):
        arrived(load_rest[1])
        field = jnp.concatenate([parts[k] for k in sorted(parts) if k[0] == g], axis=0).reshape(MINE, HIGH)
        last = jnp.zeros((MINE, LANES), F32)
        for t in range(7):
            top, rest = halves(field[:, t * LANES : (t + 1) * LANES])
            v = dot(jnp.concatenate([top, rest], axis=0), back[t * LANES : (t + 1) * LANES])
            v = v[:MINE, : 2 * LANES] + (v[MINE:, : 2 * LANES] + v[:MINE, 2 * LANES :])
            base = g * SPAN + t * LANES
            nm[:, base : base + LANES] = v[:, :LANES]
            last += v[:, LANES:]
        nm[:, g * SPAN + HIGH : (g + 1) * SPAN] = last
        cols = pl.ds(g * SPAN, SPAN)
        store(nm.at[:, cols], new_out.at[:, cols])

    def low_a(_):
        @pl.when(column_later > 0)
        def _():
            pl.semaphore_wait(column_sem, column_later)

        for k, (dy, dc) in enumerate(column):
            send("la", lw.at[ys[dy], other_core if dc else core], la.at[k], device(dy=dy, dcore=dc), LOW_A)

    def low_d(_):
        received(la, LOW_A)
        lw[y, core] += ((la[0] + la[1]) + (la[2] + la[3])) + ((la[4] + la[5]) + la[6])
        for d in (1, 2, 3):
            send("lc", lw.at[y, core, xs[d]], lc.at[d - 1], device(dx=d), LOW_C)

    def low_e(_):
        received(lc, LOW_C)
        es[...] = lw[y, core, x] + (lc[0] + lc[1] + lc[2])

        @pl.when(stack_later > 0)
        def _():
            pl.semaphore_wait(stack_sem, stack_later)

        @pl.when(core == z)
        def _():
            for d in (1, 2, 3):
                send("ld", es, le.at[d - 1], device(dzh=d), LOW_D)

        @pl.when(core != z)
        def _():
            for d in range(4):
                send("ld", es, le.at[3 + d], device(dzh=d, dz=1), LOW_D)

    def low_i(_):
        @pl.when(core == z)
        def _():
            received(le, LOW_D)
            total[y] = es[...] + ((le[0] + le[1] + le[2]) + (le[3] + le[4] + le[5] + le[6]))
            for dy, dc in column:
                send("lf", total.at[y], total.at[y], device(dy=dy, dcore=dc), LOW_F)

    def low_end():
        arrived(load_rest[1])

        @pl.when(core == z)
        def _():
            received(total.at[pl.ds(0, 3)], LOW_F)

        @pl.when(core != z)
        def _():
            received(total, LOW_F)

    normalised = set()

    def normalise(g):
        if not normalised:
            low_end()
        normalised.add(g)
        table = lambda i: back[(7 + i) * LANES : (8 + i) * LANES]
        lanes = slice(g * LANES, (g + 1) * LANES)
        mean = total[:, :, lanes].reshape(MINE, LANES) * (1.0 / N_REP)
        top, rest = halves(mean)
        pair = jnp.concatenate([top, rest], axis=0)
        squares = jnp.concatenate(halves(mean * mean), axis=0)
        for h in range(2):
            v, w = dot(pair, table(h)), dot(squares, table(4 + h))
            field = v[:MINE] + (v[MINE:] + dot(top, table(2 + h)))
            square = w[:MINE] + w[MINE:]
            base = g * SPAN + h * WIDE
            up[:, base : base + WIDE] = field * lax.rsqrt(field * field + square + EPS)
        cols = pl.ds(g * SPAN, SPAN)
        store(up.at[:, cols], upd_out.at[:, cols])

    steps = {
        "F": forward, "FL": forward_low,
        "XS": x_start, "XP": x_pass, "XC": x_cross, "XE": x_end,
        "ZS": z_start, "ZC": z_cross, "ZP": z_pass, "ZE": z_end,
        "LA": low_a, "LC": low_d, "LD": low_e, "LF": low_i,
        "N": normalise, "BK": backward,
    }
    entered = answered = False
    for name, u in PLAN:
        if not entered and name not in ("F", "FL"):
            enter()
            entered = True
        if entered and not answered and name not in ("XS", "ZS"):
            greet_others((column_sem, stack_sem), False)
            answered = True
        steps[name](u)

    all_sent("x2", xr2)
    all_sent("xa", xr2)
    all_sent("xb", xr2)
    all_sent("xz", xrz)
    all_sent("z4", zr4)
    all_sent("z2", zr2)
    all_sent("za", zr2)
    all_sent("zb", zr2)
    all_sent("la", la)
    all_sent("lc", lc)

    @pl.when(core != z)
    def _():
        all_sent("ld", le.at[pl.ds(0, 4)])

    @pl.when(core == z)
    def _():
        all_sent("ld", le.at[pl.ds(0, 3)])
        all_sent("lf", le)

    for copy in stores:
        copy.wait()


def write_out(new_in, upd_in, new_out, upd_out, sems):
    copies = []
    for k, (src, dst) in enumerate([(new_in, new_out), (upd_in, upd_out)]):
        for m in range(MATS):
            rows = pl.ds(m * OWN, OWN)
            copies.append(pltpu.make_async_copy(src.at[rows], dst.at[rows], sems.at[k, m]))
    for copy in copies:
        copy.start()
    for copy in copies:
        copy.wait()


def per_device(gradients, momentum):
    wide, back = tables()
    anywhere = pl.BlockSpec(memory_space=pl.ANY)
    new_momentum, update = pl.pallas_call(
        kernel,
        out_shape=[jax.ShapeDtypeStruct((MINE, D), F32)] * 2,
        in_specs=[anywhere] * 4,
        out_specs=[anywhere] * 2,
        scratch_shapes=[
            pltpu.VMEM((GRAD + 2 * MINE, D), BF16),
            pltpu.VMEM((MINE, D), F32),
            pltpu.VMEM(wide.shape, BF16),
            pltpu.VMEM(back.shape, BF16),
            pltpu.VMEM((len(X_UNITS), NX, NZL, 2, OWN, HIGH), F32),
            pltpu.VMEM((len(Z_UNITS), NZL, NX, 2, OWN, HIGH), F32),
            pltpu.VMEM((MATS, NZL, NX, OWN, LOW), F32),
            pltpu.VMEM((len(X_UNITS), NZL, 2, OWN, HIGH), F32),
            pltpu.VMEM((len(X_UNITS), 2, NZL, 2, OWN, HIGH), F32),
            pltpu.VMEM((len(X_UNITS), 2, OWN, HIGH), F32),
            pltpu.VMEM((len(Z_UNITS), NX, 2, OWN, HIGH), F32),
            pltpu.VMEM((len(Z_UNITS), 2, OWN, HIGH), F32),
            pltpu.VMEM((len(Z_UNITS), 2, 2, OWN, HIGH), F32),
            pltpu.VMEM((7, NX, OWN, LOW), F32),
            pltpu.VMEM((3, OWN, LOW), F32),
            pltpu.VMEM((7, OWN, LOW), F32),
            pltpu.VMEM((OWN, LOW), F32),
            pltpu.VMEM((MATS, OWN, LOW), F32),
            pltpu.VMEM((MINE, D), F32),
            pltpu.VMEM((MINE, D), F32),
            pltpu.SemaphoreType.DMA((2 * GROUPS + 3,)),
            pltpu.SemaphoreType.DMA((2 * GROUPS,)),
            pltpu.SemaphoreType.DMA((len(SENDS),)),
            pltpu.SemaphoreType.DMA((3 * len(X_UNITS) + 3 * len(Z_UNITS) + 4,)),
            pltpu.SemaphoreType.REGULAR,
            pltpu.SemaphoreType.REGULAR,
        ],
        compiler_params=pltpu.CompilerParams(
            collective_id=0, has_side_effects=True, vmem_limit_bytes=(52 * 1024 + 384) * 1024
        ),
        cost_estimate=pl.CostEstimate(flops=2_000_000_000, bytes_accessed=8_000_000, transcendentals=200_000),
    )(gradients.reshape(GRAD, D), momentum.reshape(MINE, D), wide, back)
    new_momentum, update = pl.pallas_call(
        write_out,
        out_shape=[jax.ShapeDtypeStruct((MINE, D), F32)] * 2,
        in_specs=[anywhere] * 2,
        out_specs=[anywhere] * 2,
        scratch_shapes=[pltpu.SemaphoreType.DMA((2, 4))],
        compiler_params=pltpu.CompilerParams(vmem_limit_bytes=4 * 1024 * 1024),
        cost_estimate=pl.CostEstimate(flops=0, bytes_accessed=2_600_000, transcendentals=0),
    )(new_momentum, update)
    return new_momentum.reshape(1, MATS, OWN, D), update.reshape(MATS, OWN, D)


def solution(mesh):
    return jax.shard_map(
        per_device,
        mesh=mesh,
        in_specs=(P("rep", "fsdp", None, None, None), P("rep", None, "fsdp", None)),
        out_specs=(P("rep", None, "fsdp", None), P(None, "fsdp", None)),
        check_vma=False,
    )
```

profile of v0, /device:TPU:1, one launch (start us, length us, event | category | flops | bytes accessed | tf_op | source)
XLA Modules:
  0.0 44.4 jit_solution(9709756073048123633)
XLA Ops:
  0.6 42.7 %shard_map.59 = (f32[32,5120]{1,0:T(8,128)S(1)}, f32[32,5120]{1,0:T(8,128)S(1)}) custom-call(bf16[256,5120]{1,0:T(8,128)(2,1)} %bitcast.4, f32[32,5120]{1,0:T(8,128)} %bitcast.5, bf16[2816,256]{1,0:T(8,128)(2,1)} %constant.4.clone.wide_hbm, bf16[1664,512]{1,0:T(8,128)(2,1)} %constant.5.clone.back_hbm), custom_call_target="tpu_custom_call" | custom-call | flops 2000000000 | bytes 8000000 | tf_op jit(solution)/shard_map/pallas_call | solution.py:462
  43.3 1.1 %shard_map.60 = (f32[32,5120]{1,0:T(8,128)}, f32[32,5120]{1,0:T(8,128)}) custom-call(f32[32,5120]{1,0:T(8,128)S(1)} %get-tuple-element.6.new_in, f32[32,5120]{1,0:T(8,128)S(1)} %get-tuple-element.7.upd_in), custom_call_target="tpu_custom_call" | custom-call | bytes 2600000 | tf_op jit(solution)/shard_map/pallas_call | solution.py:500
where the time goes:
time: 44.5 us; the launch traced here: 44.4 us
  Pallas kernels  43.8 us (98%)
  between operations  0.64 us (1%)
    pallas_call x1, Pallas kernels, per_device(): pl.pallas_call(kernel, out_shape=[jax.ShapeDtypeStruct((MINE, D), F32)] *...  42.7 us
    pallas_call x1, Pallas kernels, per_device(): pl.pallas_call(write_out, out_shape=[jax.ShapeDtypeStruct((MINE, D), F32)...  1.12 us

commit v1 on v0

--- a/solution.py
+++ b/solution.py
@@ -71,18 +71,31 @@
 X_UNITS = [(2, 0), (2, 2), (3, 0), (3, 2), (4, 0), (4, 2)]
 Z_UNITS = [(0, 0), (0, 2), (1, 0), (1, 2)]
 SENDS = ["x2", "xa", "xb", "xz", "z4", "z2", "za", "zb", "la", "lc", "ld", "lf"]
-PLAN = [
-    ("F", 4), ("XS", 4), ("F", 1), ("ZS", 3), ("FL", 4), ("FL", 3),
-    ("XS", 5), ("FL", 2), ("FL", 1), ("FL", 0), ("LA", 0), ("F", 3),
-    ("XS", 2), ("ZS", 2), ("F", 2), ("XS", 0), ("F", 0), ("XS", 3),
-    ("XP", 5), ("ZS", 1), ("ZS", 0), ("XP", 2), ("LC", 0), ("XS", 1),
-    ("XP", 3), ("XP", 4), ("ZC", 3), ("XP", 0), ("ZC", 1), ("LD", 0),
-    ("ZC", 2), ("XP", 1), ("XC", 2), ("XC", 3), ("XC", 5), ("XC", 4),
-    ("ZP", 3), ("ZC", 0), ("XE", 2), ("ZP", 2), ("XE", 3), ("BK", 3),
-    ("XC", 0), ("XE", 5), ("LF", 0), ("ZP", 1), ("XC", 1), ("XE", 4),
-    ("BK", 4), ("ZP", 0), ("ZE", 3), ("ZE", 2), ("BK", 1), ("XE", 1),
-    ("XE", 0), ("BK", 2), ("ZE", 1), ("ZE", 0), ("BK", 0), ("N", 3),
-    ("N", 1), ("N", 2), ("N", 0), ("N", 4),
+EARLY = [
+    ("F", 2), ("XS", 1), ("F", 1), ("ZS", 3), ("FL", 1), ("XS", 0),
+    ("F", 4), ("FL", 2), ("ZS", 2), ("XS", 4), ("FL", 4), ("FL", 0),
+    ("FL", 3), ("LA", 0), ("XS", 5), ("F", 0), ("XP", 1), ("XP", 0),
+    ("ZS", 1), ("F", 3), ("ZC", 3), ("XS", 2), ("XC", 1), ("XP", 5),
+    ("ZS", 0), ("ZP", 3), ("LC", 0), ("XP", 4), ("XP", 2), ("XS", 3),
+    ("ZC", 1), ("ZC", 2), ("LD", 0), ("XC", 0), ("XC", 5), ("ZE", 3),
+    ("XE", 1), ("XP", 3), ("XC", 4), ("ZC", 0), ("XC", 2), ("ZP", 2),
+    ("LF", 0), ("XE", 0), ("BK", 2), ("XC", 3), ("ZP", 1), ("XE", 5),
+    ("ZP", 0), ("XE", 4), ("BK", 4), ("ZE", 2), ("BK", 1), ("XE", 2),
+    ("N", 0), ("N", 1), ("N", 2), ("N", 3), ("N", 4), ("XE", 3),
+    ("BK", 3), ("ZE", 1), ("ZE", 0), ("BK", 0),
+]
+LATE = [
+    ("F", 2), ("XS", 0), ("F", 1), ("ZS", 3), ("FL", 2), ("FL", 1),
+    ("XS", 1), ("FL", 4), ("FL", 3), ("FL", 0), ("LA", 0), ("XP", 0),
+    ("F", 3), ("XS", 3), ("ZS", 2), ("XP", 1), ("F", 0), ("XS", 2),
+    ("ZS", 1), ("ZC", 3), ("F", 4), ("LC", 0), ("XS", 4), ("XP", 2),
+    ("XC", 1), ("XS", 5), ("XP", 3), ("LD", 0), ("ZC", 1), ("ZS", 0),
+    ("XC", 0), ("XE", 1), ("XP", 4), ("ZC", 2), ("XP", 5), ("ZP", 3),
+    ("XC", 2), ("LF", 0), ("ZP", 1), ("XC", 3), ("ZC", 0), ("ZP", 2),
+    ("XE", 0), ("BK", 2), ("XC", 4), ("XE", 2), ("N", 2), ("XC", 5),
+    ("N", 4), ("N", 0), ("XE", 3), ("ZP", 0), ("BK", 3), ("N", 3),
+    ("XE", 4), ("ZE", 3), ("N", 1), ("ZE", 2), ("BK", 1), ("ZE", 1),
+    ("XE", 5), ("BK", 4), ("ZE", 0), ("BK", 0),
 ]
 
 
@@ -183,7 +196,7 @@
         loads.append(copy)
         return copy
 
-    waited = set()
+    waited, ready, parts, normalised = set(), set(), {}, set()
 
     def arrived(copy):
         if id(copy) not in waited:
@@ -194,7 +207,7 @@
         cols = pl.ds(g * SPAN, SPAN)
         return load(momentum.at[:, cols], mom.at[:, cols]), load(grads.at[:, cols], xin.at[pl.ds(0, GRAD), cols])
 
-    order = [g for name, g in PLAN if name == "F"]
+    order = [g for name, g in EARLY if name == "F"]
     front = pl.ds(0, 7 * 2 * LANES)
     rest = pl.ds(7 * 2 * LANES, SPAN)
     group_loads = {order[0]: load_group(order[0])}
@@ -207,8 +220,6 @@
             group_loads[g] = load_group(g)
         load_rest.append(load(wide_hbm.at[rest], wide.at[rest]))
         load_rest.append(load(back_hbm, back))
-
-    ready = set()
 
     def prepare(g):
         if g not in ready:
@@ -299,8 +310,6 @@
         sz[u, z, xs[d]] += zr2[u]
         send("zb", sz.at[u, z, xs[d]], zab.at[u, 1], device(dx=d), ZAB + u)
 
-    parts = {}
-
     def x_end(u):
         received(xrz.at[u], XZ + u)
         parts[X_UNITS[u]] = sx[u, x, z] + xrz[u]
@@ -381,8 +390,6 @@
         @pl.when(core != z)
         def _():
             received(total, LOW_F)
-
-    normalised = set()
 
     def normalise(g):
         if not normalised:
@@ -410,38 +417,54 @@
         "LA": low_a, "LC": low_d, "LD": low_e, "LF": low_i,
         "N": normalise, "BK": backward,
     }
-    entered = answered = False
-    for name, u in PLAN:
-        if not entered and name not in ("F", "FL"):
-            enter()
-            entered = True
-        if entered and not answered and name not in ("XS", "ZS"):
-            greet_others((column_sem, stack_sem), False)
-            answered = True
-        steps[name](u)
-
-    all_sent("x2", xr2)
-    all_sent("xa", xr2)
-    all_sent("xb", xr2)
-    all_sent("xz", xrz)
-    all_sent("z4", zr4)
-    all_sent("z2", zr2)
-    all_sent("za", zr2)
-    all_sent("zb", zr2)
-    all_sent("la", la)
-    all_sent("lc", lc)
-
-    @pl.when(core != z)
+    steps[EARLY[0][0]](EARLY[0][1])
+    enter()
+    before = set(ready), set(waited)
+
+    def run(plan):
+        ready.clear()
+        ready.update(before[0])
+        waited.clear()
+        waited.update(before[1])
+        for state in (parts, normalised):
+            state.clear()
+        stores.clear()
+        answered = False
+        for name, u in plan[1:]:
+            if not answered and name not in ("XS", "ZS"):
+                greet_others((column_sem, stack_sem), False)
+                answered = True
+            steps[name](u)
+        all_sent("x2", xr2)
+        all_sent("xa", xr2)
+        all_sent("xb", xr2)
+        all_sent("xz", xrz)
+        all_sent("z4", zr4)
+        all_sent("z2", zr2)
+        all_sent("za", zr2)
+        all_sent("zb", zr2)
+        all_sent("la", la)
+        all_sent("lc", lc)
+
+        @pl.when(core != z)
+        def _():
+            all_sent("ld", le.at[pl.ds(0, 4)])
+
+        @pl.when(core == z)
+        def _():
+            all_sent("ld", le.at[pl.ds(0, 3)])
+            all_sent("lf", le)
+
+        for copy in stores:
+            copy.wait()
+
+    @pl.when(zh < 2)
     def _():
-        all_sent("ld", le.at[pl.ds(0, 4)])
-
-    @pl.when(core == z)
+        run(EARLY)
+
+    @pl.when(zh >= 2)
     def _():
-        all_sent("ld", le.at[pl.ds(0, 3)])
-        all_sent("lf", le)
-
-    for copy in stores:
-        copy.wait()
+        run(LATE)
 
 
 def write_out(new_in, upd_in, new_out, upd_out, sems):

time: 44.5 us -> 43.9 us (0.987)
  Pallas kernels: 43.8 us -> 43.1 us
    pallas_call x1, Pallas kernels: 42.7 us -> 42 us  [per_device(): pl.pallas_call(kernel, out_shape=[jax.ShapeDtypeStruct((MINE, D), F32)] *...]
where the time goes in v1:
time: 43.9 us; the launch traced here: 43.8 us
  Pallas kernels  43.1 us (98%)
  between operations  0.64 us (1%)
    pallas_call x1, Pallas kernels, per_device(): pl.pallas_call(kernel, out_shape=[jax.ShapeDtypeStruct((MINE, D), F32)] *...  42 us
    pallas_call x1, Pallas kernels, per_device(): pl.pallas_call(write_out, out_shape=[jax.ShapeDtypeStruct((MINE, D), F32)...  1.12 us

profile of v1, /device:TPU:1, one launch (start us, length us, event | category | flops | bytes accessed | tf_op | source)
XLA Modules:
  0.0 43.8 jit_solution(15857576932161001773)
XLA Ops:
  0.6 42.0 %shard_map.59 = (f32[32,5120]{1,0:T(8,128)S(1)}, f32[32,5120]{1,0:T(8,128)S(1)}) custom-call(bf16[256,5120]{1,0:T(8,128)(2,1)} %bitcast.4, f32[32,5120]{1,0:T(8,128)} %bitcast.5, bf16[2816,256]{1,0:T(8,128)(2,1)} %constant.4.clone.wide_hbm, bf16[1664,512]{1,0:T(8,128)(2,1)} %constant.5.clone.back_hbm), custom_call_target="tpu_custom_call" | custom-call | flops 2000000000 | bytes 8000000 | tf_op jit(solution)/shard_map/pallas_call | solution.py:485
  42.6 1.1 %shard_map.60 = (f32[32,5120]{1,0:T(8,128)}, f32[32,5120]{1,0:T(8,128)}) custom-call(f32[32,5120]{1,0:T(8,128)S(1)} %get-tuple-element.6.new_in, f32[32,5120]{1,0:T(8,128)S(1)} %get-tuple-element.7.upd_in), custom_call_target="tpu_custom_call" | custom-call | bytes 2600000 | tf_op jit(solution)/shard_map/pallas_call | solution.py:523

commit v2 on v1

--- a/solution.py
+++ b/solution.py
@@ -72,30 +72,30 @@
 Z_UNITS = [(0, 0), (0, 2), (1, 0), (1, 2)]
 SENDS = ["x2", "xa", "xb", "xz", "z4", "z2", "za", "zb", "la", "lc", "ld", "lf"]
 EARLY = [
-    ("F", 2), ("XS", 1), ("F", 1), ("ZS", 3), ("FL", 1), ("XS", 0),
-    ("F", 4), ("FL", 2), ("ZS", 2), ("XS", 4), ("FL", 4), ("FL", 0),
-    ("FL", 3), ("LA", 0), ("XS", 5), ("F", 0), ("XP", 1), ("XP", 0),
-    ("ZS", 1), ("F", 3), ("ZC", 3), ("XS", 2), ("XC", 1), ("XP", 5),
-    ("ZS", 0), ("ZP", 3), ("LC", 0), ("XP", 4), ("XP", 2), ("XS", 3),
-    ("ZC", 1), ("ZC", 2), ("LD", 0), ("XC", 0), ("XC", 5), ("ZE", 3),
-    ("XE", 1), ("XP", 3), ("XC", 4), ("ZC", 0), ("XC", 2), ("ZP", 2),
-    ("LF", 0), ("XE", 0), ("BK", 2), ("XC", 3), ("ZP", 1), ("XE", 5),
-    ("ZP", 0), ("XE", 4), ("BK", 4), ("ZE", 2), ("BK", 1), ("XE", 2),
-    ("N", 0), ("N", 1), ("N", 2), ("N", 3), ("N", 4), ("XE", 3),
-    ("BK", 3), ("ZE", 1), ("ZE", 0), ("BK", 0),
+    ("F", 2), ("XS", 0), ("F", 1), ("ZS", 3), ("F", 3), ("XS", 1),
+    ("XS", 2), ("ZS", 2), ("FL", 4), ("FL", 0), ("FL", 3), ("FL", 2),
+    ("FL", 1), ("LA", 0), ("XS", 3), ("F", 0), ("F", 4), ("XP", 1),
+    ("XP", 0), ("ZS", 0), ("ZC", 3), ("XS", 4), ("ZS", 1), ("LC", 0),
+    ("XS", 5), ("XP", 2), ("XP", 4), ("XP", 3), ("LD", 0), ("ZC", 2),
+    ("XP", 5), ("XC", 0), ("ZP", 3), ("XC", 1), ("ZC", 1), ("XC", 2),
+    ("XC", 3), ("ZC", 0), ("ZP", 2), ("XC", 5), ("XE", 0), ("XE", 1),
+    ("XE", 2), ("XC", 4), ("LF", 0), ("ZP", 0), ("ZE", 3), ("XE", 3),
+    ("BK", 2), ("ZP", 1), ("BK", 3), ("XE", 5), ("ZE", 2), ("BK", 1),
+    ("XE", 4), ("BK", 4), ("ZE", 0), ("N", 2), ("N", 4), ("N", 3),
+    ("N", 0), ("ZE", 1), ("BK", 0), ("N", 1),
 ]
 LATE = [
-    ("F", 2), ("XS", 0), ("F", 1), ("ZS", 3), ("FL", 2), ("FL", 1),
-    ("XS", 1), ("FL", 4), ("FL", 3), ("FL", 0), ("LA", 0), ("XP", 0),
-    ("F", 3), ("XS", 3), ("ZS", 2), ("XP", 1), ("F", 0), ("XS", 2),
-    ("ZS", 1), ("ZC", 3), ("F", 4), ("LC", 0), ("XS", 4), ("XP", 2),
-    ("XC", 1), ("XS", 5), ("XP", 3), ("LD", 0), ("ZC", 1), ("ZS", 0),
-    ("XC", 0), ("XE", 1), ("XP", 4), ("ZC", 2), ("XP", 5), ("ZP", 3),
-    ("XC", 2), ("LF", 0), ("ZP", 1), ("XC", 3), ("ZC", 0), ("ZP", 2),
-    ("XE", 0), ("BK", 2), ("XC", 4), ("XE", 2), ("N", 2), ("XC", 5),
-    ("N", 4), ("N", 0), ("XE", 3), ("ZP", 0), ("BK", 3), ("N", 3),
-    ("XE", 4), ("ZE", 3), ("N", 1), ("ZE", 2), ("BK", 1), ("ZE", 1),
-    ("XE", 5), ("BK", 4), ("ZE", 0), ("BK", 0),
+    ("F", 2), ("XS", 0), ("F", 1), ("ZS", 2), ("XS", 1), ("FL", 4),
+    ("FL", 1), ("FL", 2), ("FL", 3), ("FL", 0), ("LA", 0), ("XP", 0),
+    ("F", 4), ("XS", 5), ("ZS", 3), ("F", 0), ("F", 3), ("XP", 1),
+    ("XC", 0), ("XS", 4), ("XS", 2), ("ZS", 0), ("LC", 0), ("XS", 3),
+    ("XP", 2), ("XC", 1), ("ZC", 3), ("LD", 0), ("ZC", 0), ("ZS", 1),
+    ("XP", 4), ("ZC", 2), ("XP", 3), ("XP", 5), ("XE", 1), ("XE", 0),
+    ("XC", 2), ("ZP", 2), ("BK", 2), ("LF", 0), ("ZP", 0), ("XC", 3),
+    ("ZC", 1), ("ZP", 3), ("XC", 4), ("XC", 5), ("N", 1), ("N", 4),
+    ("N", 0), ("XE", 3), ("XE", 2), ("ZP", 1), ("ZE", 2), ("N", 2),
+    ("N", 3), ("XE", 4), ("BK", 3), ("ZE", 3), ("BK", 1), ("XE", 5),
+    ("ZE", 0), ("BK", 4), ("ZE", 1), ("BK", 0),
 ]
 
 
@@ -231,36 +231,46 @@
             xin[GRAD : GRAD + MINE, cols] = top
             xin[GRAD + MINE :, cols] = low_part
 
-    def fold(v):
+    def fold(v, count=2):
         v = v[:, :LANES] + v[:, LANES:]
-        own = v[GRAD : GRAD + MINE] + v[GRAD + MINE :]
-        return v[:GRAD].reshape(MATS, NZL, NX, OWN, LANES), own.reshape(MATS, OWN, LANES)
-
-    def forward(g):
-        prepare(g)
-        arrived(load_wide)
-        if not load_rest:
-            load_others()
+        rows, mine = count * GRAD // 2, count * MINE // 2
+        own = v[rows : rows + mine] + v[rows + mine :]
+        return v[:rows].reshape(2 * count, NZL, NX, OWN, LANES), own.reshape(2 * count, OWN, LANES)
+
+    def forward_rows(g, parts_of):
         base = g * SPAN
-        last = xin[:, base + HIGH : base + SPAN]
+
+        def rows(start):
+            cols = slice(base + start, base + start + LANES)
+            if len(parts_of) == 2:
+                return xin[:, cols]
+            h, n, k = parts_of[0], GRAD // 2, MINE // 2
+            spans = [(h * n, n), (GRAD + h * k, k), (GRAD + MINE + h * k, k)]
+            return jnp.concatenate([xin[at : at + size, cols] for at, size in spans], axis=0)
+
+        last = rows(HIGH)
         for t in range(7):
-            both = jnp.concatenate([xin[:, base + t * LANES : base + (t + 1) * LANES], last], axis=1)
-            value, own = fold(dot(both, wide[t * 2 * LANES : (t + 1) * 2 * LANES]))
+            both = jnp.concatenate([rows(t * LANES), last], axis=1)
+            value, own = fold(dot(both, wide[t * 2 * LANES : (t + 1) * 2 * LANES]), len(parts_of))
             lanes = slice(t * LANES, (t + 1) * LANES)
-            for h in range(2):
-                mats = slice(2 * h, 2 * h + 2)
+            for i, h in enumerate(parts_of):
+                mats = slice(2 * i, 2 * i + 2)
                 if (g, 2 * h) in X_UNITS:
                     u = X_UNITS.index((g, 2 * h))
                     for m in range(2):
                         for k in range(NZL):
-                            sx[u, :, k, m, :, lanes] = value[2 * h + m, k]
+                            sx[u, :, k, m, :, lanes] = value[2 * i + m, k]
                     sx[u, x, z, :, :, lanes] += own[mats]
                 else:
                     u = Z_UNITS.index((g, 2 * h))
                     for m in range(2):
                         for k in range(NZL):
-                            sz[u, k, :, m, :, lanes] = value[2 * h + m, k]
+                            sz[u, k, :, m, :, lanes] = value[2 * i + m, k]
                     sz[u, z, x, :, :, lanes] += own[mats]
+
+    def forward(g):
+        prepare(g)
+        forward_rows(g, (0, 1))
 
     def forward_low(g):
         prepare(g)
@@ -417,7 +427,11 @@
         "LA": low_a, "LC": low_d, "LD": low_e, "LF": low_i,
         "N": normalise, "BK": backward,
     }
-    steps[EARLY[0][0]](EARLY[0][1])
+    first = EARLY[0][1]
+    prepare(first)
+    arrived(load_wide)
+    load_others()
+    forward_rows(first, (0,))
     enter()
     before = set(ready), set(waited)
 
@@ -435,6 +449,8 @@
                 greet_others((column_sem, stack_sem), False)
                 answered = True
             steps[name](u)
+            if (name, u) == plan[1]:
+                forward_rows(first, (1,))
         all_sent("x2", xr2)
         all_sent("xa", xr2)
         all_sent("xb", xr2)

time: 43.9 us -> 43.5 us (level)
  no operation moved by 1% of the time
where the time goes in v2:
time: 43.5 us; the launch traced here: 43.4 us
  Pallas kernels  42.8 us (98%)
  between operations  0.64 us (1%)
    pallas_call x1, Pallas kernels, per_device(): pl.pallas_call(kernel, out_shape=[jax.ShapeDtypeStruct((MINE, D), F32)] *...  41.7 us
    pallas_call x1, Pallas kernels, per_device(): pl.pallas_call(write_out, out_shape=[jax.ShapeDtypeStruct((MINE, D), F32)...  1.12 us

profile of v2, /device:TPU:1, one launch (start us, length us, event | category | flops | bytes accessed | tf_op | source)
XLA Modules:
  0.0 43.4 jit_solution(8310463877330709051)
XLA Ops:
  0.6 41.7 %shard_map.59 = (f32[32,5120]{1,0:T(8,128)S(1)}, f32[32,5120]{1,0:T(8,128)S(1)}) custom-call(bf16[256,5120]{1,0:T(8,128)(2,1)} %bitcast.4, f32[32,5120]{1,0:T(8,128)} %bitcast.5, bf16[2816,256]{1,0:T(8,128)(2,1)} %constant.4.clone.wide_hbm, bf16[1664,512]{1,0:T(8,128)(2,1)} %constant.5.clone.back_hbm), custom_call_target="tpu_custom_call" | custom-call | flops 2000000000 | bytes 8000000 | tf_op jit(solution)/shard_map/pallas_call | solution.py:501
  42.3 1.1 %shard_map.60 = (f32[32,5120]{1,0:T(8,128)}, f32[32,5120]{1,0:T(8,128)}) custom-call(f32[32,5120]{1,0:T(8,128)S(1)} %get-tuple-element.6.new_in, f32[32,5120]{1,0:T(8,128)S(1)} %get-tuple-element.7.upd_in), custom_call_target="tpu_custom_call" | custom-call | bytes 2600000 | tf_op jit(solution)/shard_map/pallas_call | solution.py:539

commit v3 on v2

--- a/solution.py
+++ b/solution.py
@@ -72,30 +72,30 @@
 Z_UNITS = [(0, 0), (0, 2), (1, 0), (1, 2)]
 SENDS = ["x2", "xa", "xb", "xz", "z4", "z2", "za", "zb", "la", "lc", "ld", "lf"]
 EARLY = [
-    ("F", 2), ("XS", 0), ("F", 1), ("ZS", 3), ("F", 3), ("XS", 1),
-    ("XS", 2), ("ZS", 2), ("FL", 4), ("FL", 0), ("FL", 3), ("FL", 2),
-    ("FL", 1), ("LA", 0), ("XS", 3), ("F", 0), ("F", 4), ("XP", 1),
-    ("XP", 0), ("ZS", 0), ("ZC", 3), ("XS", 4), ("ZS", 1), ("LC", 0),
-    ("XS", 5), ("XP", 2), ("XP", 4), ("XP", 3), ("LD", 0), ("ZC", 2),
-    ("XP", 5), ("XC", 0), ("ZP", 3), ("XC", 1), ("ZC", 1), ("XC", 2),
-    ("XC", 3), ("ZC", 0), ("ZP", 2), ("XC", 5), ("XE", 0), ("XE", 1),
-    ("XE", 2), ("XC", 4), ("LF", 0), ("ZP", 0), ("ZE", 3), ("XE", 3),
-    ("BK", 2), ("ZP", 1), ("BK", 3), ("XE", 5), ("ZE", 2), ("BK", 1),
-    ("XE", 4), ("BK", 4), ("ZE", 0), ("N", 2), ("N", 4), ("N", 3),
-    ("N", 0), ("ZE", 1), ("BK", 0), ("N", 1),
+    ("F", 2), ("XS", 1), ("F", 1), ("ZS", 3), ("FL", 1), ("XS", 0),
+    ("F", 4), ("FL", 2), ("ZS", 2), ("XS", 4), ("FL", 4), ("FL", 0),
+    ("FL", 3), ("LA", 0), ("XS", 5), ("F", 0), ("XP", 1), ("XP", 0),
+    ("ZS", 1), ("F", 3), ("ZC", 3), ("XS", 2), ("XC", 1), ("XP", 5),
+    ("ZS", 0), ("ZP", 3), ("LC", 0), ("XP", 4), ("XP", 2), ("XS", 3),
+    ("ZC", 1), ("ZC", 2), ("LD", 0), ("XC", 0), ("XC", 5), ("ZE", 3),
+    ("XE", 1), ("XP", 3), ("XC", 4), ("ZC", 0), ("XC", 2), ("ZP", 2),
+    ("XE", 0), ("BK", 2), ("XC", 3), ("ZP", 1), ("XE", 5), ("ZP", 0),
+    ("LF", 0), ("XE", 4), ("BK", 4), ("ZE", 2), ("BK", 1), ("XE", 2),
+    ("XE", 3), ("BK", 3), ("ZE", 1), ("ZE", 0), ("BK", 0), ("N", 0),
+    ("N", 1), ("N", 2), ("N", 3), ("N", 4),
 ]
 LATE = [
-    ("F", 2), ("XS", 0), ("F", 1), ("ZS", 2), ("XS", 1), ("FL", 4),
-    ("FL", 1), ("FL", 2), ("FL", 3), ("FL", 0), ("LA", 0), ("XP", 0),
-    ("F", 4), ("XS", 5), ("ZS", 3), ("F", 0), ("F", 3), ("XP", 1),
-    ("XC", 0), ("XS", 4), ("XS", 2), ("ZS", 0), ("LC", 0), ("XS", 3),
-    ("XP", 2), ("XC", 1), ("ZC", 3), ("LD", 0), ("ZC", 0), ("ZS", 1),
-    ("XP", 4), ("ZC", 2), ("XP", 3), ("XP", 5), ("XE", 1), ("XE", 0),
-    ("XC", 2), ("ZP", 2), ("BK", 2), ("LF", 0), ("ZP", 0), ("XC", 3),
-    ("ZC", 1), ("ZP", 3), ("XC", 4), ("XC", 5), ("N", 1), ("N", 4),
-    ("N", 0), ("XE", 3), ("XE", 2), ("ZP", 1), ("ZE", 2), ("N", 2),
-    ("N", 3), ("XE", 4), ("BK", 3), ("ZE", 3), ("BK", 1), ("XE", 5),
-    ("ZE", 0), ("BK", 4), ("ZE", 1), ("BK", 0),
+    ("F", 2), ("XS", 0), ("F", 1), ("ZS", 3), ("FL", 2), ("FL", 1),
+    ("XS", 1), ("FL", 4), ("FL", 3), ("FL", 0), ("LA", 0), ("XP", 0),
+    ("F", 3), ("XS", 3), ("ZS", 2), ("XP", 1), ("F", 0), ("XS", 2),
+    ("ZS", 1), ("ZC", 3), ("F", 4), ("LC", 0), ("XS", 4), ("XP", 2),
+    ("XC", 1), ("XS", 5), ("XP", 3), ("LD", 0), ("ZC", 1), ("ZS", 0),
+    ("XC", 0), ("XE", 1), ("XP", 4), ("ZC", 2), ("XP", 5), ("ZP", 3),
+    ("XC", 2), ("LF", 0), ("ZP", 1), ("XC", 3), ("ZC", 0), ("ZP", 2),
+    ("XE", 0), ("BK", 2), ("XC", 4), ("XE", 2), ("N", 2), ("XC", 5),
+    ("N", 4), ("N", 0), ("XE", 3), ("ZP", 0), ("BK", 3), ("N", 3),
+    ("XE", 4), ("ZE", 3), ("N", 1), ("ZE", 2), ("BK", 1), ("ZE", 1),
+    ("XE", 5), ("BK", 4), ("ZE", 0), ("BK", 0),
 ]
 
 
@@ -431,8 +431,6 @@
     prepare(first)
     arrived(load_wide)
     load_others()
-    forward_rows(first, (0,))
-    enter()
     before = set(ready), set(waited)
 
     def run(plan):
@@ -444,13 +442,16 @@
             state.clear()
         stores.clear()
         answered = False
+        half = X_UNITS[plan[1][1]][1] // 2
+        forward_rows(first, (half,))
+        enter()
         for name, u in plan[1:]:
             if not answered and name not in ("XS", "ZS"):
                 greet_others((column_sem, stack_sem), False)
                 answered = True
             steps[name](u)
             if (name, u) == plan[1]:
-                forward_rows(first, (1,))
+                forward_rows(first, (1 - half,))
         all_sent("x2", xr2)
         all_sent("xa", xr2)
         all_sent("xb", xr2)

time: 43.5 us -> 43.6 us (level)
  no operation moved by 1% of the time
where the time goes in v3:
time: 43.6 us; the launch traced here: 43.5 us
  Pallas kernels  42.9 us (98%)
  between operations  0.64 us (1%)
    pallas_call x1, Pallas kernels, per_device(): pl.pallas_call(kernel, out_shape=[jax.ShapeDtypeStruct((MINE, D), F32)] *...  41.8 us
    pallas_call x1, Pallas kernels, per_device(): pl.pallas_call(write_out, out_shape=[jax.ShapeDtypeStruct((MINE, D), F32)...  1.12 us

profile of v3, /device:TPU:1, one launch (start us, length us, event | category | flops | bytes accessed | tf_op | source)
XLA Modules:
  0.0 43.5 jit_solution(2073448428325178289)
XLA Ops:
  0.6 41.8 %shard_map.59 = (f32[32,5120]{1,0:T(8,128)S(1)}, f32[32,5120]{1,0:T(8,128)S(1)}) custom-call(bf16[256,5120]{1,0:T(8,128)(2,1)} %bitcast.4, f32[32,5120]{1,0:T(8,128)} %bitcast.5, bf16[2816,256]{1,0:T(8,128)(2,1)} %constant.4.clone.wide_hbm, bf16[1664,512]{1,0:T(8,128)(2,1)} %constant.5.clone.back_hbm), custom_call_target="tpu_custom_call" | custom-call | flops 2000000000 | bytes 8000000 | tf_op jit(solution)/shard_map/pallas_call | solution.py:502
  42.4 1.1 %shard_map.60 = (f32[32,5120]{1,0:T(8,128)}, f32[32,5120]{1,0:T(8,128)}) custom-call(f32[32,5120]{1,0:T(8,128)S(1)} %get-tuple-element.6.new_in, f32[32,5120]{1,0:T(8,128)S(1)} %get-tuple-element.7.upd_in), custom_call_target="tpu_custom_call" | custom-call | bytes 2600000 | tf_op jit(solution)/shard_map/pallas_call | solution.py:540

commit v4 on v3

--- a/solution.py
+++ b/solution.py
@@ -79,10 +79,9 @@
     ("ZS", 0), ("ZP", 3), ("LC", 0), ("XP", 4), ("XP", 2), ("XS", 3),
     ("ZC", 1), ("ZC", 2), ("LD", 0), ("XC", 0), ("XC", 5), ("ZE", 3),
     ("XE", 1), ("XP", 3), ("XC", 4), ("ZC", 0), ("XC", 2), ("ZP", 2),
-    ("XE", 0), ("BK", 2), ("XC", 3), ("ZP", 1), ("XE", 5), ("ZP", 0),
-    ("LF", 0), ("XE", 4), ("BK", 4), ("ZE", 2), ("BK", 1), ("XE", 2),
-    ("XE", 3), ("BK", 3), ("ZE", 1), ("ZE", 0), ("BK", 0), ("N", 0),
-    ("N", 1), ("N", 2), ("N", 3), ("N", 4),
+    ("XE", 0), ("BK", 2), ("XC", 3), ("ZP", 1), ("LF", 0), ("XE", 5),
+    ("ZP", 0), ("XE", 4), ("BK", 4), ("ZE", 2), ("BK", 1), ("XE", 2),
+    ("N", 0), ("XE", 3), ("BK", 3), ("ZE", 1), ("ZE", 0), ("BK", 0),
 ]
 LATE = [
     ("F", 2), ("XS", 0), ("F", 1), ("ZS", 3), ("FL", 2), ("FL", 1),
@@ -92,10 +91,9 @@
     ("XC", 1), ("XS", 5), ("XP", 3), ("LD", 0), ("ZC", 1), ("ZS", 0),
     ("XC", 0), ("XE", 1), ("XP", 4), ("ZC", 2), ("XP", 5), ("ZP", 3),
     ("XC", 2), ("LF", 0), ("ZP", 1), ("XC", 3), ("ZC", 0), ("ZP", 2),
-    ("XE", 0), ("BK", 2), ("XC", 4), ("XE", 2), ("N", 2), ("XC", 5),
-    ("N", 4), ("N", 0), ("XE", 3), ("ZP", 0), ("BK", 3), ("N", 3),
-    ("XE", 4), ("ZE", 3), ("N", 1), ("ZE", 2), ("BK", 1), ("ZE", 1),
-    ("XE", 5), ("BK", 4), ("ZE", 0), ("BK", 0),
+    ("XE", 0), ("BK", 2), ("XC", 4), ("XE", 2), ("XC", 5), ("XE", 3),
+    ("ZP", 0), ("N", 0), ("BK", 3), ("XE", 4), ("ZE", 3), ("ZE", 2),
+    ("BK", 1), ("ZE", 1), ("XE", 5), ("BK", 4), ("ZE", 0), ("BK", 0),
 ]
 
 
@@ -196,7 +194,7 @@
         loads.append(copy)
         return copy
 
-    waited, ready, parts, normalised = set(), set(), {}, set()
+    waited, ready, parts = set(), set(), {}
 
     def arrived(copy):
         if id(copy) not in waited:
@@ -401,24 +399,25 @@
         def _():
             received(total, LOW_F)
 
-    def normalise(g):
-        if not normalised:
-            low_end()
-        normalised.add(g)
+    def normalise(_):
+        low_end()
         table = lambda i: back[(7 + i) * LANES : (8 + i) * LANES]
-        lanes = slice(g * LANES, (g + 1) * LANES)
-        mean = total[:, :, lanes].reshape(MINE, LANES) * (1.0 / N_REP)
+        count = GROUPS * MINE
+        mean = jnp.concatenate(
+            [total[:, :, g * LANES : (g + 1) * LANES].reshape(MINE, LANES) for g in range(GROUPS)], axis=0
+        ) * (1.0 / N_REP)
         top, rest = halves(mean)
         pair = jnp.concatenate([top, rest], axis=0)
         squares = jnp.concatenate(halves(mean * mean), axis=0)
         for h in range(2):
             v, w = dot(pair, table(h)), dot(squares, table(4 + h))
-            field = v[:MINE] + (v[MINE:] + dot(top, table(2 + h)))
-            square = w[:MINE] + w[MINE:]
-            base = g * SPAN + h * WIDE
-            up[:, base : base + WIDE] = field * lax.rsqrt(field * field + square + EPS)
-        cols = pl.ds(g * SPAN, SPAN)
-        store(up.at[:, cols], upd_out.at[:, cols])
+            field = v[:count] + (v[count:] + dot(top, table(2 + h)))
+            square = w[:count] + w[count:]
+            value = field * lax.rsqrt(field * field + square + EPS)
+            for g in range(GROUPS):
+                base = g * SPAN + h * WIDE
+                up[:, base : base + WIDE] = value[g * MINE : (g + 1) * MINE]
+        store(up, upd_out)
 
     steps = {
         "F": forward, "FL": forward_low,
@@ -438,8 +437,7 @@
         ready.update(before[0])
         waited.clear()
         waited.update(before[1])
-        for state in (parts, normalised):
-            state.clear()
+        parts.clear()
         stores.clear()
         answered = False
         half = X_UNITS[plan[1][1]][1] // 2
@@ -475,11 +473,11 @@
         for copy in stores:
             copy.wait()
 
-    @pl.when(zh < 2)
+    @pl.when(zh == 0)
     def _():
         run(EARLY)
 
-    @pl.when(zh >= 2)
+    @pl.when(zh > 0)
     def _():
         run(LATE)
 
@@ -526,7 +524,7 @@
             pltpu.VMEM((MINE, D), F32),
             pltpu.VMEM((MINE, D), F32),
             pltpu.SemaphoreType.DMA((2 * GROUPS + 3,)),
-            pltpu.SemaphoreType.DMA((2 * GROUPS,)),
+            pltpu.SemaphoreType.DMA((GROUPS + 1,)),
             pltpu.SemaphoreType.DMA((len(SENDS),)),
             pltpu.SemaphoreType.DMA((3 * len(X_UNITS) + 3 * len(Z_UNITS) + 4,)),
             pltpu.SemaphoreType.REGULAR,

time: 43.6 us -> 43.1 us (0.989)
  Pallas kernels: 42.9 us -> 42.3 us
    pallas_call x1, Pallas kernels: 41.8 us -> 41.2 us  [per_device(): pl.pallas_call(kernel, out_shape=[jax.ShapeDtypeStruct((MINE, D), F32)] *...]
where the time goes in v4:
time: 43.1 us; the launch traced here: 43 us
  Pallas kernels  42.3 us (98%)
  between operations  0.64 us (1%)
    pallas_call x1, Pallas kernels, per_device(): pl.pallas_call(kernel, out_shape=[jax.ShapeDtypeStruct((MINE, D), F32)] *...  41.2 us
    pallas_call x1, Pallas kernels, per_device(): pl.pallas_call(write_out, out_shape=[jax.ShapeDtypeStruct((MINE, D), F32)...  1.12 us

profile of v4, /device:TPU:1, one launch (start us, length us, event | category | flops | bytes accessed | tf_op | source)
XLA Modules:
  0.0 43.0 jit_solution(13247699328694026470)
XLA Ops:
  0.6 41.2 %shard_map.59 = (f32[32,5120]{1,0:T(8,128)S(1)}, f32[32,5120]{1,0:T(8,128)S(1)}) custom-call(bf16[256,5120]{1,0:T(8,128)(2,1)} %bitcast.4, f32[32,5120]{1,0:T(8,128)} %bitcast.5, bf16[2816,256]{1,0:T(8,128)(2,1)} %constant.4.clone.wide_hbm, bf16[1664,512]{1,0:T(8,128)(2,1)} %constant.5.clone.back_hbm), custom_call_target="tpu_custom_call" | custom-call | flops 2000000000 | bytes 8000000 | tf_op jit(solution)/shard_map/pallas_call | solution.py:500
  41.9 1.1 %shard_map.60 = (f32[32,5120]{1,0:T(8,128)}, f32[32,5120]{1,0:T(8,128)}) custom-call(f32[32,5120]{1,0:T(8,128)S(1)} %get-tuple-element.6.new_in, f32[32,5120]{1,0:T(8,128)S(1)} %get-tuple-element.7.upd_in), custom_call_target="tpu_custom_call" | custom-call | bytes 2600000 | tf_op jit(solution)/shard_map/pallas_call | solution.py:538

commit v5 on v4

--- a/solution.py
+++ b/solution.py
@@ -81,14 +81,14 @@
     ("XE", 1), ("XP", 3), ("XC", 4), ("ZC", 0), ("XC", 2), ("ZP", 2),
     ("XE", 0), ("BK", 2), ("XC", 3), ("ZP", 1), ("LF", 0), ("XE", 5),
     ("ZP", 0), ("XE", 4), ("BK", 4), ("ZE", 2), ("BK", 1), ("XE", 2),
-    ("N", 0), ("XE", 3), ("BK", 3), ("ZE", 1), ("ZE", 0), ("BK", 0),
+    ("XE", 3), ("BK", 3), ("ZE", 1), ("ZE", 0), ("BK", 0), ("N", 0),
 ]
 LATE = [
     ("F", 2), ("XS", 0), ("F", 1), ("ZS", 3), ("FL", 2), ("FL", 1),
     ("XS", 1), ("FL", 4), ("FL", 3), ("FL", 0), ("LA", 0), ("XP", 0),
     ("F", 3), ("XS", 3), ("ZS", 2), ("XP", 1), ("F", 0), ("XS", 2),
-    ("ZS", 1), ("ZC", 3), ("F", 4), ("LC", 0), ("XS", 4), ("XP", 2),
-    ("XC", 1), ("XS", 5), ("XP", 3), ("LD", 0), ("ZC", 1), ("ZS", 0),
+    ("ZS", 1), ("ZC", 3), ("LC", 0), ("F", 4), ("XS", 4), ("XP", 2),
+    ("XC", 1), ("LD", 0), ("XS", 5), ("XP", 3), ("ZC", 1), ("ZS", 0),
     ("XC", 0), ("XE", 1), ("XP", 4), ("ZC", 2), ("XP", 5), ("ZP", 3),
     ("XC", 2), ("LF", 0), ("ZP", 1), ("XC", 3), ("ZC", 0), ("ZP", 2),
     ("XE", 0), ("BK", 2), ("XC", 4), ("XE", 2), ("XC", 5), ("XE", 3),

time: 43.1 us -> 42.4 us (0.984)
  Pallas kernels: 42.3 us -> 41.7 us
    pallas_call x1, Pallas kernels: 41.2 us -> 40.5 us  [per_device(): pl.pallas_call(kernel, out_shape=[jax.ShapeDtypeStruct((MINE, D), F32)] *...]
where the time goes in v5:
time: 42.4 us; the launch traced here: 42.3 us
  Pallas kernels  41.7 us (98%)
  between operations  0.64 us (2%)
    pallas_call x1, Pallas kernels, per_device(): pl.pallas_call(kernel, out_shape=[jax.ShapeDtypeStruct((MINE, D), F32)] *...  40.5 us
    pallas_call x1, Pallas kernels, per_device(): pl.pallas_call(write_out, out_shape=[jax.ShapeDtypeStruct((MINE, D), F32)...  1.12 us

profile of v5, /device:TPU:1, one launch (start us, length us, event | category | flops | bytes accessed | tf_op | source)
XLA Modules:
  0.0 42.3 jit_solution(10827813557015728269)
XLA Ops:
  0.6 40.5 %shard_map.59 = (f32[32,5120]{1,0:T(8,128)S(1)}, f32[32,5120]{1,0:T(8,128)S(1)}) custom-call(bf16[256,5120]{1,0:T(8,128)(2,1)} %bitcast.4, f32[32,5120]{1,0:T(8,128)} %bitcast.5, bf16[2816,256]{1,0:T(8,128)(2,1)} %constant.4.clone.wide_hbm, bf16[1664,512]{1,0:T(8,128)(2,1)} %constant.5.clone.back_hbm), custom_call_target="tpu_custom_call" | custom-call | flops 2000000000 | bytes 8000000 | tf_op jit(solution)/shard_map/pallas_call | solution.py:500
  41.2 1.1 %shard_map.60 = (f32[32,5120]{1,0:T(8,128)}, f32[32,5120]{1,0:T(8,128)}) custom-call(f32[32,5120]{1,0:T(8,128)S(1)} %get-tuple-element.6.new_in, f32[32,5120]{1,0:T(8,128)S(1)} %get-tuple-element.7.upd_in), custom_call_target="tpu_custom_call" | custom-call | bytes 2600000 | tf_op jit(solution)/shard_map/pallas_call | solution.py:538

commit v6 on v5

--- a/solution.py
+++ b/solution.py
@@ -79,15 +79,15 @@
     ("ZS", 0), ("ZP", 3), ("LC", 0), ("XP", 4), ("XP", 2), ("XS", 3),
     ("ZC", 1), ("ZC", 2), ("LD", 0), ("XC", 0), ("XC", 5), ("ZE", 3),
     ("XE", 1), ("XP", 3), ("XC", 4), ("ZC", 0), ("XC", 2), ("ZP", 2),
-    ("XE", 0), ("BK", 2), ("XC", 3), ("ZP", 1), ("LF", 0), ("XE", 5),
+    ("XE", 0), ("BK", 2), ("LF", 0), ("XC", 3), ("ZP", 1), ("XE", 5),
     ("ZP", 0), ("XE", 4), ("BK", 4), ("ZE", 2), ("BK", 1), ("XE", 2),
     ("XE", 3), ("BK", 3), ("ZE", 1), ("ZE", 0), ("BK", 0), ("N", 0),
 ]
 LATE = [
     ("F", 2), ("XS", 0), ("F", 1), ("ZS", 3), ("FL", 2), ("FL", 1),
     ("XS", 1), ("FL", 4), ("FL", 3), ("FL", 0), ("LA", 0), ("XP", 0),
-    ("F", 3), ("XS", 3), ("ZS", 2), ("XP", 1), ("F", 0), ("XS", 2),
-    ("ZS", 1), ("ZC", 3), ("LC", 0), ("F", 4), ("XS", 4), ("XP", 2),
+    ("F", 3), ("XS", 3), ("ZS", 2), ("XP", 1), ("F", 0), ("LC", 0),
+    ("XS", 2), ("ZS", 1), ("ZC", 3), ("F", 4), ("XS", 4), ("XP", 2),
     ("XC", 1), ("LD", 0), ("XS", 5), ("XP", 3), ("ZC", 1), ("ZS", 0),
     ("XC", 0), ("XE", 1), ("XP", 4), ("ZC", 2), ("XP", 5), ("ZP", 3),
     ("XC", 2), ("LF", 0), ("ZP", 1), ("XC", 3), ("ZC", 0), ("ZP", 2),

time: 42.4 us -> 44 us (1.038)
  the two profiles are of different devices: /device:TPU:1 before, /device:TPU:64 now
where the time goes in v6:
time: 44 us; the launch traced here: 43.9 us
  Pallas kernels  43.3 us (98%)
  between operations  0.64 us (1%)
    pallas_call x1, Pallas kernels, per_device(): pl.pallas_call(kernel, out_shape=[jax.ShapeDtypeStruct((MINE, D), F32)] *...  42.1 us
    pallas_call x1, Pallas kernels, per_device(): pl.pallas_call(write_out, out_shape=[jax.ShapeDtypeStruct((MINE, D), F32)...  1.12 us

profile of v6, /device:TPU:64, one launch (start us, length us, event | category | flops | bytes accessed | tf_op | source)
XLA Modules:
  0.0 43.9 jit_solution(9171145885653121582)
XLA Ops:
  0.6 42.1 %shard_map.59 = (f32[32,5120]{1,0:T(8,128)S(1)}, f32[32,5120]{1,0:T(8,128)S(1)}) custom-call(bf16[256,5120]{1,0:T(8,128)(2,1)} %bitcast.4, f32[32,5120]{1,0:T(8,128)} %bitcast.5, bf16[2816,256]{1,0:T(8,128)(2,1)} %constant.4.clone.wide_hbm, bf16[1664,512]{1,0:T(8,128)(2,1)} %constant.5.clone.back_hbm), custom_call_target="tpu_custom_call" | custom-call | flops 2000000000 | bytes 8000000 | tf_op jit(solution)/shard_map/pallas_call | solution.py:500
  42.8 1.1 %shard_map.60 = (f32[32,5120]{1,0:T(8,128)}, f32[32,5120]{1,0:T(8,128)}) custom-call(f32[32,5120]{1,0:T(8,128)S(1)} %get-tuple-element.6.new_in, f32[32,5120]{1,0:T(8,128)S(1)} %get-tuple-element.7.upd_in), custom_call_target="tpu_custom_call" | custom-call | bytes 2600000 | tf_op jit(solution)/shard_map/pallas_call | solution.py:538

commit v7 on v5

--- a/solution.py
+++ b/solution.py
@@ -79,7 +79,7 @@
     ("ZS", 0), ("ZP", 3), ("LC", 0), ("XP", 4), ("XP", 2), ("XS", 3),
     ("ZC", 1), ("ZC", 2), ("LD", 0), ("XC", 0), ("XC", 5), ("ZE", 3),
     ("XE", 1), ("XP", 3), ("XC", 4), ("ZC", 0), ("XC", 2), ("ZP", 2),
-    ("XE", 0), ("BK", 2), ("XC", 3), ("ZP", 1), ("LF", 0), ("XE", 5),
+    ("LF", 0), ("XE", 0), ("BK", 2), ("XC", 3), ("ZP", 1), ("XE", 5),
     ("ZP", 0), ("XE", 4), ("BK", 4), ("ZE", 2), ("BK", 1), ("XE", 2),
     ("XE", 3), ("BK", 3), ("ZE", 1), ("ZE", 0), ("BK", 0), ("N", 0),
 ]

time: 42.4 us -> 40.6 us (0.958)
  Pallas kernels: 41.7 us -> 39.6 us
    pallas_call x1, Pallas kernels: 40.5 us -> 38.5 us  [per_device(): pl.pallas_call(kernel, out_shape=[jax.ShapeDtypeStruct((MINE, D), F32)] *...]
where the time goes in v7:
time: 40.6 us; the launch traced here: 40.3 us
  Pallas kernels  39.6 us (98%)
  between operations  0.64 us (2%)
    pallas_call x1, Pallas kernels, per_device(): pl.pallas_call(kernel, out_shape=[jax.ShapeDtypeStruct((MINE, D), F32)] *...  38.5 us
    pallas_call x1, Pallas kernels, per_device(): pl.pallas_call(write_out, out_shape=[jax.ShapeDtypeStruct((MINE, D), F32)...  1.12 us

profile of v7, /device:TPU:1, one launch (start us, length us, event | category | flops | bytes accessed | tf_op | source)
XLA Modules:
  0.0 40.3 jit_solution(929435398387387760)
XLA Ops:
  0.6 38.5 %shard_map.59 = (f32[32,5120]{1,0:T(8,128)S(1)}, f32[32,5120]{1,0:T(8,128)S(1)}) custom-call(bf16[256,5120]{1,0:T(8,128)(2,1)} %bitcast.4, f32[32,5120]{1,0:T(8,128)} %bitcast.5, bf16[2816,256]{1,0:T(8,128)(2,1)} %constant.4.clone.wide_hbm, bf16[1664,512]{1,0:T(8,128)(2,1)} %constant.5.clone.back_hbm), custom_call_target="tpu_custom_call" | custom-call | flops 2000000000 | bytes 8000000 | tf_op jit(solution)/shard_map/pallas_call | solution.py:500
  39.2 1.1 %shard_map.60 = (f32[32,5120]{1,0:T(8,128)}, f32[32,5120]{1,0:T(8,128)}) custom-call(f32[32,5120]{1,0:T(8,128)S(1)} %get-tuple-element.6.new_in, f32[32,5120]{1,0:T(8,128)S(1)} %get-tuple-element.7.upd_in), custom_call_target="tpu_custom_call" | custom-call | bytes 2600000 | tf_op jit(solution)/shard_map/pallas_call | solution.py:538

commit v8 on v7

--- a/solution.py
+++ b/solution.py
@@ -81,7 +81,7 @@
     ("XE", 1), ("XP", 3), ("XC", 4), ("ZC", 0), ("XC", 2), ("ZP", 2),
     ("LF", 0), ("XE", 0), ("BK", 2), ("XC", 3), ("ZP", 1), ("XE", 5),
     ("ZP", 0), ("XE", 4), ("BK", 4), ("ZE", 2), ("BK", 1), ("XE", 2),
-    ("XE", 3), ("BK", 3), ("ZE", 1), ("ZE", 0), ("BK", 0), ("N", 0),
+    ("XE", 3), ("BK", 3), ("N", 0), ("ZE", 1), ("ZE", 0), ("BK", 0),
 ]
 LATE = [
     ("F", 2), ("XS", 0), ("F", 1), ("ZS", 3), ("FL", 2), ("FL", 1),

time: 40.6 us -> 40.7 us (level)
  no operation moved by 1% of the time
where the time goes in v8:
time: 40.7 us; the launch traced here: 40.6 us
  Pallas kernels  40 us (98%)
  between operations  0.64 us (2%)
    pallas_call x1, Pallas kernels, per_device(): pl.pallas_call(kernel, out_shape=[jax.ShapeDtypeStruct((MINE, D), F32)] *...  38.9 us
    pallas_call x1, Pallas kernels, per_device(): pl.pallas_call(write_out, out_shape=[jax.ShapeDtypeStruct((MINE, D), F32)...  1.12 us

profile of v8, /device:TPU:1, one launch (start us, length us, event | category | flops | bytes accessed | tf_op | source)
XLA Modules:
  0.0 40.6 jit_solution(9786630463092606113)
XLA Ops:
  0.6 38.9 %shard_map.59 = (f32[32,5120]{1,0:T(8,128)S(1)}, f32[32,5120]{1,0:T(8,128)S(1)}) custom-call(bf16[256,5120]{1,0:T(8,128)(2,1)} %bitcast.4, f32[32,5120]{1,0:T(8,128)} %bitcast.5, bf16[2816,256]{1,0:T(8,128)(2,1)} %constant.4.clone.wide_hbm, bf16[1664,512]{1,0:T(8,128)(2,1)} %constant.5.clone.back_hbm), custom_call_target="tpu_custom_call" | custom-call | flops 2000000000 | bytes 8000000 | tf_op jit(solution)/shard_map/pallas_call | solution.py:500
  39.5 1.1 %shard_map.60 = (f32[32,5120]{1,0:T(8,128)}, f32[32,5120]{1,0:T(8,128)}) custom-call(f32[32,5120]{1,0:T(8,128)S(1)} %get-tuple-element.6.new_in, f32[32,5120]{1,0:T(8,128)S(1)} %get-tuple-element.7.upd_in), custom_call_target="tpu_custom_call" | custom-call | bytes 2600000 | tf_op jit(solution)/shard_map/pallas_call | solution.py:538
